TPU v7x, 512 devices: a whole 4x8x8 slice. The times are simulated.
512 devices in a mesh: ctx: 64 (over y, x, core), head: 8 (over z).
Axes of the slice: x: 4, y: 8, z: 8, core: 2. Of those that a mesh axis runs over, the one named last changes fastest.
Arguments:
- query_rows: bfloat16 [16384, 5120], P('ctx', 'head'), may hold values from -7.5 to 7.5
- gate_rows: bfloat16 [16384, 5120], P('ctx', 'head'), may hold values from -4 to 12
- value_rows: bfloat16 [16384, 5120], P('ctx', 'head'), may hold values from -6 to 6
- upstream_rows: bfloat16 [16384, 5120], P('ctx', 'head'), may hold values from -6 to 6
- row_map: int32 [16384], P('ctx'), may hold values from 0 to 16383, as said below
- doc_lengths: int32 [64], replicated, may hold values from 1 to 2048, 16384 in all
- entry_state: float32 [64, 40, 128, 128], P('ctx', 'head'), may hold values from -1.75 to 1.75
- lower_bound: float32 [5120], P('head'), may hold values from 0.3 to 0.7
- norm_gain: float32 [5120], P('head'), may hold values from 0.1 to 1.9
Outputs:
- query_grad: bfloat16 [16384, 5120], P('ctx', 'head')
- gate_grad: bfloat16 [16384, 5120], P('ctx', 'head')
- value_grad: bfloat16 [16384, 5120], P('ctx', 'head')
Inputs may be any that keep to these rules, and one draw needn't show every extreme that they name: `row_map`: every loader row appears exactly once; the 256 rows of one balanced shard take at most 8 rows from any one loader shard, and that most is reached. `doc_lengths`: the lengths sum to 16384.
All inputs are finite; a program needn't handle non-finite values.
Results may differ from a plain program's by a relative error of at most 0.0022.
Values may be sent and summed in bfloat16 or wider, within the bound.
A program may use at most 128 MiB of HBM per device.

v0:
```python
import functools

import jax
import jax.numpy as jnp
from jax import lax
from jax.experimental import pallas as pl
from jax.experimental.pallas import tpu as pltpu
from jax.sharding import PartitionSpec as P

BLOCK = 128
LANES = 128
DOC_MOST = 2048
EPSILON = 1e-06
MESH = pl.DeviceIdType.MESH
BF = jnp.bfloat16
F32 = jnp.float32
NN = (((1,), (0,)), ((), ()))
NT = (((1,), (1,)), ((), ()))


def dot(a, b, dims):
    return lax.dot_general(a, b, dims, preferred_element_type=F32)


def cat(parts, axis):
    return jnp.concatenate(parts, axis=axis)


def halves(x):
    high = x.astype(BF)
    return high, (x - high.astype(F32)).astype(BF)


def thirds(x):
    high = x.astype(BF)
    rest = x - high.astype(F32)
    middle = rest.astype(BF)
    return high, middle, (rest - middle.astype(F32)).astype(BF)


def nn3(a, b):
    return dot(cat([a[0], a[0], a[1]], 1), cat([b[0], b[1], b[0]], 0), NN)


def nt3(a, b):
    return dot(cat([a[0], a[0], a[1]], 1), cat([b[0], b[1], b[0]], 1), NT)


def nn2(a, exact):
    return dot(cat(a, 1), cat([exact, exact], 0), NN)


def nt2(a, exact):
    return dot(cat(a, 1), cat([exact, exact], 1), NT)


def exact_nn2(exact, b):
    return dot(cat([exact, exact], 1), cat(b, 0), NN)


def iota(shape, axis):
    return lax.broadcasted_iota(jnp.int32, shape, axis)


def one(mask):
    return jnp.where(mask, 1.0, 0.0).astype(F32)


def column(row):
    parts = [
        jnp.broadcast_to(row[:, at : at + LANES], (LANES, LANES)).T
        for at in range(0, row.shape[1], LANES)
    ]
    return cat(parts, 0) if len(parts) > 1 else parts[0]


def widen(col, width):
    return cat([col] * (width // LANES), 1)


def peer(me, k, count):
    if count != 64:
        return lax.rem(me + k, count)
    dy, rest = lax.rem(k, 8), lax.div(k, 8)
    dx, dc = lax.div(rest, 2), lax.rem(rest, 2)
    y = lax.rem(lax.div(me, 8) + dy, 8)
    x = lax.rem(lax.rem(lax.div(me, 2), 4) + dx, 4)
    core = lax.rem(lax.rem(me, 2) + dc, 2)
    return (y * 4 + x) * 2 + core


def kernel(
    sizes,
    small_ref,
    q_ref,
    p_ref,
    v_ref,
    y_ref,
    entry_ref,
    bound_ref,
    gain_ref,
    dq_ref,
    dp_ref,
    dv_ref,
    req_send,
    req_recv,
    row_send,
    row_recv,
    dq_send,
    dq_recv,
    dvp_send,
    dvp_recv,
    sum_send,
    sum_recv,
    tot_send,
    tot_recv,
    car_send,
    car_recv,
    stat_send,
    stat_recv,
    gather_ref,
    settle_ref,
    place_ref,
    back_ref,
    shared_ref,
    shared_t_ref,
    valid_ref,
    last_ref,
    through_ref,
    q_bal,
    v_bal,
    y_bal,
    sig_ref,
    forget_ref,
    store_ref,
    eq_ref,
    ek_ref,
    tail_ref,
    qd_ref,
    kd_ref,
    score_ref,
    weight_ref,
    state_ref,
    factor_ref,
    back_state_ref,
    out_ref,
    dq_bal,
    dk_bal,
    dv_bal,
    square_ref,
    cross_ref,
    send_sem,
    recv_sem,
):
    count, head_count, rows, heads, cap, group, chunks = sizes
    slots = count * cap
    blocks = rows // BLOCK
    part = LANES // group
    me = lax.axis_index("ctx")
    plane = lax.axis_index("head")
    base = me * rows

    def to_ctx(src, dst, sem, d):
        return pltpu.make_async_remote_copy(
            src_ref=src,
            dst_ref=dst,
            send_sem=send_sem.at[sem],
            recv_sem=recv_sem.at[sem],
            device_id={"ctx": d},
            device_id_type=MESH,
        )

    def drain(view, sems, sem):
        pltpu.make_async_copy(view, view, sems.at[sem]).wait()

    REQ, STAT, SUM, TOT, CAR, DQ, ROWS = 0, 1, 2, 3, 4, 5, 6
    DVP = ROWS + len(chunks)

    barrier = pltpu.get_barrier_semaphore()

    def greet(k, carry):
        pl.semaphore_signal(
            barrier, inc=1, device_id={"ctx": peer(me, k, count)}, device_id_type=MESH
        )
        return carry

    def greet_plane(k, carry):
        pl.semaphore_signal(
            barrier,
            inc=1,
            device_id={"head": lax.rem(plane + k, head_count)},
            device_id_type=MESH,
        )
        return carry

    lax.fori_loop(1, count, greet, 0)
    lax.fori_loop(1, head_count, greet_plane, 0)

    small = small_ref[...].astype(F32)
    map_row = cat([small[b : b + 1] for b in range(blocks)], 1)
    source_row = jnp.floor(map_row * (1.0 / rows))
    local_row = map_row - source_row * rows
    source_col = column(source_row)
    local_col = column(local_row)
    same = (widen(source_col, rows) == source_row) & (
        iota((rows, rows), 0) < iota((rows, rows), 1)
    )
    rank_row = jnp.sum(one(same), axis=0, keepdims=True)
    slot_row = source_row * cap + rank_row
    slot_col = column(slot_row)
    back_ref[...] = one(iota((slots, rows), 0).astype(F32) == slot_row).astype(BF)
    place_ref[...] = one(
        iota((rows, slots), 1).astype(F32) == widen(slot_col, slots)
    ).astype(BF)
    asked_mine = dot(back_ref[...], (local_col + 1.0).astype(BF), NN) - 1.0
    req_send[...] = asked_mine.reshape(count, cap, LANES)

    pl.semaphore_wait(barrier, count - 1 + head_count - 1)

    def ask(k, carry):
        d = peer(me, k, count)
        to_ctx(req_send.at[d], req_recv.at[me], REQ, d).start()
        return carry

    lax.fori_loop(1, count, ask, 0)
    req_recv[me] = req_send[me]

    length_col = column(small[blocks : blocks + 1])
    ends_row = jnp.sum(
        jnp.where(iota((LANES, LANES), 0) <= iota((LANES, LANES), 1), length_col, 0.0),
        axis=0,
        keepdims=True,
    )
    ends_col = column(ends_row)
    position = (iota((1, rows), 1) + base).astype(F32)
    document_row = jnp.sum(one(widen(ends_col, rows) <= position), axis=0, keepdims=True)
    document_col = column(document_row)
    before = (iota((1, LANES), 1) * 0 + (base - 1)).astype(F32)
    before = jnp.where(
        before < 0.0, -1.0, jnp.sum(one(ends_col <= before), axis=0, keepdims=True)
    )
    for b in range(blocks):
        at = slice(b * BLOCK, (b + 1) * BLOCK)
        previous = before if b == 0 else document_col[b * BLOCK - 1 : b * BLOCK]
        final = document_col[(b + 1) * BLOCK - 1 : (b + 1) * BLOCK]
        alike = document_col[at] == document_row[:, at]
        earlier = iota((BLOCK, BLOCK), 0) >= iota((BLOCK, BLOCK), 1)
        later = iota((BLOCK, BLOCK), 0) <= iota((BLOCK, BLOCK), 1)
        shared_ref[b] = one(alike & earlier)
        shared_t_ref[b] = one(alike & later)
        valid_ref[b] = one(document_col[at] == previous)
        last_ref[b] = one(document_col[at] == final)
        through_ref[pl.ds(b, 1)] = one(previous == final)

    def wait_all(view, sem):
        drain(view, recv_sem, sem)

    wait_all(req_recv.at[pl.ds(0, count - 1)], REQ)
    asked = req_recv[...].reshape(slots, LANES)
    gather = cat(
        [
            one(asked == (iota((slots, LANES), 1) + b * LANES).astype(F32))
            for b in range(blocks)
        ],
        1,
    )
    gather_ref[...] = gather.astype(BF)

    step_slots = min(slots, 128)
    step_peers = step_slots // cap
    for number, (first, past) in enumerate(chunks):

        def pack(h, carry):
            at = pl.ds(pl.multiple_of(h * LANES, LANES), LANES)
            wide = cat([q_ref[:, at], p_ref[:, at], v_ref[:, at], y_ref[:, at]], 1)
            for piece in range(slots // step_slots):
                picked = dot(
                    gather_ref[piece * step_slots : (piece + 1) * step_slots], wide, NN
                )
                slab = cat(
                    [
                        picked[:, a * LANES : (a + 1) * LANES].reshape(step_peers, cap, LANES)
                        for a in range(4)
                    ],
                    1,
                )
                row_send[h, piece * step_peers : (piece + 1) * step_peers] = slab.astype(BF)
            return carry

        lax.fori_loop(first, past, pack, 0)

        def serve(k, carry):
            d = peer(me, k, count)
            span = pl.ds(first, past - first)
            to_ctx(row_send.at[span, d], row_recv.at[span, me], ROWS + number, d).start()
            return carry

        lax.fori_loop(1, count, serve, 0)

    def own(h, carry):
        row_recv[h, me] = row_send[h, me]
        return carry

    lax.fori_loop(0, heads, own, 0)
    settle_ref[...] = gather.T.astype(BF)

    square_ref[...] = jnp.zeros_like(square_ref)
    cross_ref[...] = jnp.zeros_like(cross_ref)
    lower = one(iota((BLOCK, BLOCK), 0) >= iota((BLOCK, BLOCK), 1)).astype(BF)
    lower3 = cat([lower, lower, lower], 1)

    def unslab(slab, parts):
        wide = slab.astype(F32)
        return cat(
            [
                wide[:, a * cap : (a + 1) * cap].reshape(slots, LANES).astype(BF)
                for a in range(parts)
            ],
            1,
        )

    def forward(h, carry):
        balanced = dot(place_ref[...], unslab(row_recv[h], 4), NN)
        bound = bound_ref[pl.ds(h, 1)]
        gain = gain_ref[pl.ds(h, 1)]
        state = entry_ref[0, h].T
        for b in range(blocks):
            at = slice(b * BLOCK, (b + 1) * BLOCK)
            q, p, v, y = [balanced[at, a * LANES : (a + 1) * LANES] for a in range(4)]
            v_exact = v.astype(BF)
            sig = jax.nn.sigmoid(p)
            forget = bound + (1.0 - bound) * sig
            store = 1.0 - forget
            decay = dot(lower3, cat(thirds(jnp.log(forget)), 0), NN)
            total = decay[BLOCK - 1 : BLOCK]
            eq = jnp.exp(decay)
            ek = jnp.exp(-decay)
            tail = jnp.exp(total - decay) * last_ref[b]
            factor = through_ref[pl.ds(b, 1)] * jnp.exp(total)
            qd = q * eq
            kd = store * ek
            qd2 = halves(qd)
            scores = nt3(qd2, halves(kd)) * shared_ref[b]
            out = nn2(halves(scores), v_exact) + valid_ref[b] * nt3(qd2, halves(state))
            state_ref[h, b] = state
            state = state * factor + exact_nn2(v.T.astype(BF), halves(store * tail))
            square_ref[at] += out * out
            cross_ref[at] += gain * y * out
            q_bal[h, b] = q.astype(BF)
            v_bal[h, b] = v_exact
            y_bal[h, b] = y.astype(BF)
            sig_ref[h, b] = sig
            forget_ref[h, b] = forget
            store_ref[h, b] = store
            eq_ref[h, b] = eq
            ek_ref[h, b] = ek
            tail_ref[h, b] = tail
            qd_ref[h, b] = qd
            kd_ref[h, b] = kd
            score_ref[h, b] = scores
            factor_ref[h, b] = factor
            out_ref[h, b] = out
        state_ref[h, blocks] = state
        return carry

    for number, (first, past) in enumerate(chunks):
        wait_all(
            row_recv.at[pl.ds(first, past - first), pl.ds(0, count - 1)], ROWS + number
        )
        lax.fori_loop(first, past, forward, 0)

    ones = jnp.ones((8, 3 * LANES), BF)
    squares = dot(ones, cat(thirds(square_ref[...]), 1), NT)
    crosses = dot(ones, cat(thirds(cross_ref[...]), 1), NT)
    stat_send[...] = jnp.where(iota((8, rows), 0) < 4, squares, crosses)

    def share(k, carry):
        pltpu.make_async_remote_copy(
            src_ref=stat_send,
            dst_ref=stat_recv.at[plane],
            send_sem=send_sem.at[STAT],
            recv_sem=recv_sem.at[STAT],
            device_id={"head": lax.rem(plane + k, head_count)},
            device_id_type=MESH,
        ).start()
        return carry

    lax.fori_loop(1, head_count, share, 0)
    stat_recv[plane] = stat_send[...]
    sum_send[...] = jnp.zeros_like(sum_send)
    if head_count > 1:
        wait_all(stat_recv.at[pl.ds(0, head_count - 1)], STAT)
    stats = jnp.sum(stat_recv[...], axis=0)
    width = float(head_count * heads * LANES)
    inverse = lax.rsqrt(stats[0:1] / width + EPSILON)
    slope = inverse * inverse * inverse * (stats[4:5] / width)
    square_ref[...] = column(inverse)
    cross_ref[...] = column(slope)

    def summarize(h, carry):
        gain = gain_ref[pl.ds(h, 1)]
        back = []
        for b in range(blocks):
            at = slice(b * BLOCK, (b + 1) * BLOCK)
            g = square_ref[at] * gain * y_bal[h, b].astype(F32) - out_ref[h, b] * cross_ref[at]
            out_ref[h, b] = g
            back.append(nn3(halves((g * valid_ref[b]).T), halves(qd_ref[h, b])))
            back_state_ref[h, b] = back[b]
        summary = back[blocks - 1]
        decay = factor_ref[h, blocks - 1]
        for b in reversed(range(blocks - 1)):
            summary = back[b] + factor_ref[h, b] * summary
            decay = decay * factor_ref[h, b]
        sum_send[:, h] = summary.reshape(group, part, LANES)
        sum_send[:, heads, pl.ds(h, 1)] = jnp.broadcast_to(decay[None], (group, 1, LANES))
        return carry

    lax.fori_loop(0, heads, summarize, 0)

    first_member = lax.div(me, group) * group
    mine = lax.rem(me, group)

    def member(k):
        return lax.rem(mine + k, group)

    def give_summary(k, carry):
        m = member(k)
        to_ctx(sum_send.at[m], sum_recv.at[mine], SUM, first_member + m).start()
        return carry

    lax.fori_loop(1, group, give_summary, 0)
    sum_recv[mine] = sum_send[mine]

    def query_side(h, carry):
        for b in range(blocks):
            g2 = halves(out_ref[h, b])
            weights = nt2(g2, v_bal[h, b]) * shared_ref[b]
            weight_ref[h, b] = weights
            dq = nn3(halves(weights), halves(kd_ref[h, b]))
            dq = dq + valid_ref[b] * nn3(g2, halves(state_ref[h, b]))
            dq_bal[h, b] = dq * eq_ref[h, b]
        return carry

    lax.fori_loop(0, heads, query_side, 0)

    def column_of(ref, h):
        return cat([ref[h, b].astype(BF) for b in range(blocks)], 0)

    halfway = (heads + 1) // 2
    for c in range(halfway):
        pair = [column_of(dq_bal, c)]
        if halfway + c < heads:
            pair.append(column_of(dq_bal, halfway + c))
        else:
            pair.append(jnp.zeros((rows, LANES), BF))
        sent = dot(back_ref[...], cat(pair, 1), NN)
        slab = cat(
            [sent[:, a * LANES : (a + 1) * LANES].reshape(count, cap, LANES) for a in range(2)],
            1,
        )
        dq_send[c] = slab.astype(BF)

    def home_queries(k, carry):
        d = peer(me, k, count)
        to_ctx(
            dq_send.at[pl.ds(0, halfway), d], dq_recv.at[pl.ds(0, halfway), me], DQ, d
        ).start()
        return carry

    wait_all(sum_recv.at[pl.ds(0, group - 1)], SUM)
    lax.fori_loop(1, count, home_queries, 0)
    for c in range(halfway):
        dq_recv[c, me] = dq_send[c, me]

    def scan(h, carry):
        total = jnp.zeros((part, LANES), F32)
        for m in reversed(range(group)):
            total = sum_recv[m, h] + sum_recv[m, heads, pl.ds(h, 1)] * total
        tot_send[h] = total
        return carry

    lax.fori_loop(0, heads, scan, 0)
    groups = count // group
    if groups > 1:
        to_ctx(tot_send, tot_recv, TOT, lax.rem(me + count - group, count)).start()

    def key_side(h, carry):
        for b in range(blocks):
            dk_bal[h, b] = ek_ref[h, b] * nn3(
                halves(weight_ref[h, b].T), halves(qd_ref[h, b])
            )
            dv_bal[h, b] = nn3(halves(score_ref[h, b].T), halves(out_ref[h, b]))
        return carry

    if groups > 1:
        wait_all(tot_recv, TOT)

    def carries(h, carry):
        if groups > 1:
            total = tot_recv[h] * jnp.where(first_member + group == count, 0.0, 1.0)
        else:
            total = jnp.zeros((part, LANES), F32)
        for m in reversed(range(group)):
            car_send[m, h] = total
            total = sum_recv[m, h] + sum_recv[m, heads, pl.ds(h, 1)] * total
        return carry

    lax.fori_loop(0, heads, carries, 0)

    def give_carry(k, carry):
        m = member(k)
        to_ctx(car_send.at[m], car_recv.at[mine], CAR, first_member + m).start()
        return carry

    lax.fori_loop(1, group, give_carry, 0)
    car_recv[mine] = car_send[mine]
    lax.fori_loop(0, heads, key_side, 0)
    wait_all(car_recv.at[pl.ds(0, group - 1)], CAR)

    def finish(h, carry):
        bound = bound_ref[pl.ds(h, 1)]
        incoming = car_recv[:, h].reshape(LANES, LANES)
        pairs = [None] * blocks
        for b in reversed(range(blocks)):
            incoming2 = halves(incoming)
            tail = tail_ref[h, b]
            store = store_ref[h, b]
            sig = sig_ref[h, b]
            dv = dv_bal[h, b] + nt3(halves(store * tail), incoming2)
            dk = dk_bal[h, b] + tail * exact_nn2(v_bal[h, b], incoming2)
            mixture = q_bal[h, b].astype(F32) * dq_bal[h, b] - store * dk
            reach = shared_t_ref[b].astype(BF)
            slope = dot(cat([reach, reach, reach], 1), cat(thirds(mixture), 0), NN)
            slope = slope + last_ref[b] * jnp.sum(
                incoming * state_ref[h, b + 1], axis=0, keepdims=True
            )
            dp = (slope / forget_ref[h, b] - dk) * (1.0 - bound) * sig * (1.0 - sig)
            pairs[b] = cat([dv.astype(BF), dp.astype(BF)], 1)
            if b:
                incoming = back_state_ref[h, b] + factor_ref[h, b] * incoming
        sent = dot(back_ref[...], cat(pairs, 0), NN)
        slab = cat(
            [sent[:, a * LANES : (a + 1) * LANES].reshape(count, cap, LANES) for a in range(2)],
            1,
        )
        dvp_send[h] = slab.astype(BF)
        dvp_recv[h, me] = dvp_send[h, me]
        return carry

    for number, (first, past) in enumerate(chunks):
        lax.fori_loop(first, past, finish, 0)

        def home(k, carry):
            d = peer(me, k, count)
            span = pl.ds(first, past - first)
            to_ctx(dvp_send.at[span, d], dvp_recv.at[span, me], DVP + number, d).start()
            return carry

        lax.fori_loop(1, count, home, 0)

    wait_all(dq_recv.at[pl.ds(0, halfway), pl.ds(0, count - 1)], DQ)
    for c in range(halfway):
        rows_home = dot(settle_ref[...], unslab(dq_recv[c], 2), NN).astype(BF)
        for a in range(2):
            h = c + a * halfway
            if h < heads:
                dq_ref[:, h * LANES : (h + 1) * LANES] = rows_home[:, a * LANES : (a + 1) * LANES]

    def settle(h, carry):
        rows_home = dot(settle_ref[...], unslab(dvp_recv[h], 2), NN).astype(BF)
        at = pl.ds(pl.multiple_of(h * LANES, LANES), LANES)
        dv_ref[:, at] = rows_home[:, :LANES]
        dp_ref[:, at] = rows_home[:, LANES:]
        return carry

    for number, (first, past) in enumerate(chunks):
        span = pl.ds(first, past - first)
        wait_all(dvp_recv.at[span, pl.ds(0, count - 1)], DVP + number)
        lax.fori_loop(first, past, settle, 0)

    drain(req_send.at[pl.ds(0, count - 1)], send_sem, REQ)
    if head_count > 1:
        drain(stat_recv.at[pl.ds(0, head_count - 1)], send_sem, STAT)
    drain(sum_send.at[pl.ds(0, group - 1)], send_sem, SUM)
    if groups > 1:
        drain(tot_send, send_sem, TOT)
    drain(car_send.at[pl.ds(0, group - 1)], send_sem, CAR)
    drain(dq_send.at[pl.ds(0, halfway), pl.ds(0, count - 1)], send_sem, DQ)
    for number, (first, past) in enumerate(chunks):
        span = pl.ds(first, past - first)
        drain(row_send.at[span, pl.ds(0, count - 1)], send_sem, ROWS + number)
        drain(dvp_send.at[span, pl.ds(0, count - 1)], send_sem, DVP + number)


def body(
    count,
    head_count,
    query_rows,
    gate_rows,
    value_rows,
    upstream_rows,
    row_map,
    doc_lengths,
    entry_state,
    lower_bound,
    norm_gain,
):
    rows = row_map.shape[0]
    heads = entry_state.shape[1]
    cap = 2 * rows // count
    slots = count * cap
    blocks = rows // BLOCK
    group = DOC_MOST // rows
    chunks = tuple((h, h + 1) for h in range(heads))
    sizes = (count, head_count, rows, heads, cap, group, chunks)
    small = jnp.concatenate([row_map, doc_lengths])
    small = jnp.pad(small, (0, 8 * LANES - small.shape[0])).reshape(8, LANES)
    part = LANES // group
    halfway = (heads + 1) // 2
    vmem = pltpu.VMEM
    per_block = (heads, blocks, BLOCK, LANES)
    semaphores = 6 + 2 * len(chunks)
    scratch = [
        vmem((count, cap, LANES), F32),
        vmem((count, cap, LANES), F32),
        vmem((heads, count, 4 * cap, LANES), BF),
        vmem((heads, count, 4 * cap, LANES), BF),
        vmem((halfway, count, 2 * cap, LANES), BF),
        vmem((halfway, count, 2 * cap, LANES), BF),
        vmem((heads, count, 2 * cap, LANES), BF),
        vmem((heads, count, 2 * cap, LANES), BF),
        vmem((group, heads + 1, part, LANES), F32),
        vmem((group, heads + 1, part, LANES), F32),
        vmem((heads, part, LANES), F32),
        vmem((heads, part, LANES), F32),
        vmem((group, heads, part, LANES), F32),
        vmem((group, heads, part, LANES), F32),
        vmem((8, rows), F32),
        vmem((head_count, 8, rows), F32),
        vmem((slots, rows), BF),
        vmem((rows, slots), BF),
        vmem((rows, slots), BF),
        vmem((slots, rows), BF),
        vmem((blocks, BLOCK, BLOCK), F32),
        vmem((blocks, BLOCK, BLOCK), F32),
        vmem((blocks, BLOCK, LANES), F32),
        vmem((blocks, BLOCK, LANES), F32),
        vmem((blocks, LANES), F32),
        vmem(per_block, BF),
        vmem(per_block, BF),
        vmem(per_block, BF),
        vmem(per_block, F32),
        vmem(per_block, F32),
        vmem(per_block, F32),
        vmem(per_block, F32),
        vmem(per_block, F32),
        vmem(per_block, F32),
        vmem(per_block, F32),
        vmem(per_block, F32),
        vmem(per_block, F32),
        vmem(per_block, F32),
        vmem((heads, blocks + 1, LANES, LANES), F32),
        vmem((heads, blocks, 1, LANES), F32),
        vmem((heads, blocks, LANES, LANES), F32),
        vmem(per_block, F32),
        vmem(per_block, F32),
        vmem(per_block, F32),
        vmem(per_block, F32),
        vmem((rows, LANES), F32),
        vmem((rows, LANES), F32),
        pltpu.SemaphoreType.DMA((semaphores,)),
        pltpu.SemaphoreType.DMA((semaphores,)),
    ]
    whole = pl.BlockSpec(memory_space=pltpu.VMEM)
    shape = jax.ShapeDtypeStruct(query_rows.shape, BF)
    return pl.pallas_call(
        functools.partial(kernel, sizes),
        out_shape=(shape, shape, shape),
        in_specs=[whole] * 8,
        out_specs=(whole, whole, whole),
        scratch_shapes=scratch,
        compiler_params=pltpu.CompilerParams(
            collective_id=0, has_side_effects=True, vmem_limit_bytes=56 << 20
        ),
    )(
        small,
        query_rows,
        gate_rows,
        value_rows,
        upstream_rows,
        entry_state,
        lower_bound.reshape(heads, LANES),
        norm_gain.reshape(heads, LANES),
    )


def solution(mesh):
    placed = (
        P("ctx", "head"),
        P("ctx", "head"),
        P("ctx", "head"),
        P("ctx", "head"),
        P("ctx"),
        P(),
        P("ctx", "head", None, None),
        P("head"),
        P("head"),
    )
    return jax.shard_map(
        functools.partial(body, mesh.shape["ctx"], mesh.shape["head"]),
        mesh=mesh,
        in_specs=placed,
        out_specs=(P("ctx", "head"), P("ctx", "head"), P("ctx", "head")),
        check_vma=False,
    )
```

profile of v0, /device:TPU:1, one launch (start us, length us, event | category | flops | bytes accessed | tf_op | source)
XLA Modules:
  0.0 167.3 jit_solution(5654689594019845053)
XLA Ops:
  0.6 0.0 copy-start.2
  0.6 0.0 copy-start.3
  0.7 0.7 copy-done.2
  1.3 0.0 copy-done.3
  1.3 0.6 pad_bitcast_fusion.small_ref
  1.9 161.8 %shard_map.112 = (bf16[256,640]{1,0:T(8,128)(2,1)}, bf16[256,640]{1,0:T(8,128)(2,1)}, bf16[256,640]{1,0:T(8,128)(2,1)}) custom-call(s32[8,128]{1,0:T(8,128)} %pad_bitcast_fusion.small_ref, bf16[256,640]{1,0:T(8,128)(2,1)} %q_ref.1, bf16[256,640]{1,0:T(8,128)(2,1)} %p_ref.1, bf16[256,640]{1,0:T(8,128)(2,1)} %v_ref.1, bf16[256,640]{1,0:T(8,128)(2,1)} %y_ref.1, ...), custom_call_target="tpu_custom_call" | custom-call | tf_op jit(solution)/shard_map/pallas_call | solution.py:676
  163.7 0.0 copy-start.1
  163.8 1.8 %copy.15 = bf16[256,640]{1,0:T(8,128)(2,1)} copy(bf16[256,640]{1,0:T(8,128)(2,1)} %get-tuple-element.6) | data formatting | bytes 655360
  165.5 0.0 copy-done.1
  165.5 0.0 copy-start
  165.5 0.7 copy.16
  166.3 0.4 copy-done
  166.6 0.7 copy.17
  (1 shorter events, 0.0 us)
Async XLA Ops:
  0.6 0.7 copy-start.2
  0.6 0.7 copy-start.3
  163.7 1.8 %copy-start.1 = (bf16[256,640]{1,0:T(8,128)(2,1)S(1)}, bf16[256,640]{1,0:T(8,128)(2,1)}, u32[]{:S(2)}) copy-start(bf16[256,640]{1,0:T(8,128)(2,1)} %get-tuple-element.7) | copy-start | bytes 983044
  165.5 1.1 copy-start
where the time goes:
time: 168 us; the launch traced here: 167 us
  Pallas kernels  162 us (96%)
  local copies, waits for them, and re-layouts  4.85 us (3%)
    pallas_call x1, Pallas kernels, body(): pl.pallas_call(functools.partial(kernel, sizes), out_shape=(shape, shape,...  162 us
    unnamed x11, local copies, waits for them, and re-layouts  4.25 us

commit v1 on v0

--- a/solution.py
+++ b/solution.py
@@ -78,20 +78,33 @@
     return cat([col] * (width // LANES), 1)
 
 
-def peer(me, k, count):
+def spread(me, count, start):
     if count != 64:
-        return lax.rem(me + k, count)
-    dy, rest = lax.rem(k, 8), lax.div(k, 8)
-    dx, dc = lax.div(rest, 2), lax.rem(rest, 2)
-    y = lax.rem(lax.div(me, 8) + dy, 8)
-    x = lax.rem(lax.rem(lax.div(me, 2), 4) + dx, 4)
-    core = lax.rem(lax.rem(me, 2) + dc, 2)
-    return (y * 4 + x) * 2 + core
+
+        def one_of(k, carry):
+            start(lax.rem(me + k, count))
+            return carry
+
+        lax.fori_loop(1, count, one_of, 0)
+        return
+    y, w = lax.div(me, 8), lax.rem(me, 8)
+
+    def along_y(w_there, first):
+        for dy in range(first, 8):
+            start(lax.rem(y + dy, 8) * 8 + w_there)
+
+    def across(dw, carry):
+        along_y(lax.rem(w + dw, 8), 0)
+        return carry
+
+    along_y(w, 1)
+    lax.fori_loop(1, 8, across, 0)
 
 
 def kernel(
     sizes,
-    small_ref,
+    map_ref,
+    length_ref,
     q_ref,
     p_ref,
     v_ref,
@@ -99,9 +112,7 @@
     entry_ref,
     bound_ref,
     gain_ref,
-    dq_ref,
-    dp_ref,
-    dv_ref,
+    grad_ref,
     req_send,
     req_recv,
     row_send,
@@ -133,13 +144,17 @@
     sig_ref,
     forget_ref,
     store_ref,
-    eq_ref,
     ek_ref,
     tail_ref,
     qd_ref,
-    kd_ref,
-    score_ref,
-    weight_ref,
+    score_t_ref,
+    up_t_ref,
+    out_t_ref,
+    up_weight_ref,
+    out_weight_ref,
+    up_query_ref,
+    out_query_ref,
+    scale_ref,
     state_ref,
     factor_ref,
     back_state_ref,
@@ -173,16 +188,20 @@
     def drain(view, sems, sem):
         pltpu.make_async_copy(view, view, sems.at[sem]).wait()
 
-    REQ, STAT, SUM, TOT, CAR, DQ, ROWS = 0, 1, 2, 3, 4, 5, 6
+    leaving, due = [], []
+
+    def note(sending, receiving, sem):
+        leaving.append((sending, sem))
+        due.append((receiving, sem))
+
+    def arrive():
+        view, sem = due.pop(0)
+        drain(view, recv_sem, sem)
+
+    REQ, STAT, SUM, TOT, CAR, DQ, ROWS = 0, 1, 2, 3, 4, 5, 8
     DVP = ROWS + len(chunks)
 
     barrier = pltpu.get_barrier_semaphore()
-
-    def greet(k, carry):
-        pl.semaphore_signal(
-            barrier, inc=1, device_id={"ctx": peer(me, k, count)}, device_id_type=MESH
-        )
-        return carry
 
     def greet_plane(k, carry):
         pl.semaphore_signal(
@@ -193,39 +212,45 @@
         )
         return carry
 
-    lax.fori_loop(1, count, greet, 0)
+    spread(
+        me,
+        count,
+        lambda d: pl.semaphore_signal(
+            barrier, inc=1, device_id={"ctx": d}, device_id_type=MESH
+        ),
+    )
     lax.fori_loop(1, head_count, greet_plane, 0)
 
-    small = small_ref[...].astype(F32)
-    map_row = cat([small[b : b + 1] for b in range(blocks)], 1)
+    map_row = cat([map_ref[b : b + 1] for b in range(blocks)], 1).astype(F32)
     source_row = jnp.floor(map_row * (1.0 / rows))
-    local_row = map_row - source_row * rows
+    local_col = column(map_row - source_row * rows)
     source_col = column(source_row)
-    local_col = column(local_row)
     same = (widen(source_col, rows) == source_row) & (
         iota((rows, rows), 0) < iota((rows, rows), 1)
     )
     rank_row = jnp.sum(one(same), axis=0, keepdims=True)
     slot_row = source_row * cap + rank_row
-    slot_col = column(slot_row)
     back_ref[...] = one(iota((slots, rows), 0).astype(F32) == slot_row).astype(BF)
+    asked_mine = dot(back_ref[...], (local_col + 1.0).astype(BF), NN)
+    own_lane = iota((count, cap, LANES), 1) == iota((count, cap, LANES), 2)
+    req_send[...] = jnp.sum(
+        jnp.where(own_lane, asked_mine.reshape(count, cap, LANES), 0.0), axis=1, keepdims=True
+    )
+
+    pl.semaphore_wait(barrier, count - 1 + head_count - 1)
+    others = pl.ds(0, count - 1)
+    spread(
+        me, count, lambda d: to_ctx(req_send.at[d], req_recv.at[me], REQ, d).start()
+    )
+    note(req_send.at[others], req_recv.at[others], REQ)
+    req_recv[me] = req_send[me]
+
     place_ref[...] = one(
-        iota((rows, slots), 1).astype(F32) == widen(slot_col, slots)
+        iota((rows, slots), 1).astype(F32) == widen(column(slot_row), slots)
     ).astype(BF)
-    asked_mine = dot(back_ref[...], (local_col + 1.0).astype(BF), NN) - 1.0
-    req_send[...] = asked_mine.reshape(count, cap, LANES)
-
-    pl.semaphore_wait(barrier, count - 1 + head_count - 1)
-
-    def ask(k, carry):
-        d = peer(me, k, count)
-        to_ctx(req_send.at[d], req_recv.at[me], REQ, d).start()
-        return carry
-
-    lax.fori_loop(1, count, ask, 0)
-    req_recv[me] = req_send[me]
-
-    length_col = column(small[blocks : blocks + 1])
+
+    lengths = length_ref[...].astype(F32)
+    length_col = column(cat([lengths, jnp.zeros((1, LANES - lengths.shape[1]), F32)], 1))
     ends_row = jnp.sum(
         jnp.where(iota((LANES, LANES), 0) <= iota((LANES, LANES), 1), length_col, 0.0),
         axis=0,
@@ -252,14 +277,13 @@
         last_ref[b] = one(document_col[at] == final)
         through_ref[pl.ds(b, 1)] = one(previous == final)
 
-    def wait_all(view, sem):
-        drain(view, recv_sem, sem)
-
-    wait_all(req_recv.at[pl.ds(0, count - 1)], REQ)
-    asked = req_recv[...].reshape(slots, LANES)
+    arrive()
+    asked = jnp.broadcast_to(req_recv[...], (count, cap, LANES))
+    asked = jnp.where(own_lane, asked, 0.0).reshape(slots, LANES).astype(BF)
+    asked = dot(asked, jnp.ones((LANES, LANES), BF), NN)
     gather = cat(
         [
-            one(asked == (iota((slots, LANES), 1) + b * LANES).astype(F32))
+            one(asked == (iota((slots, LANES), 1) + (b * LANES + 1)).astype(F32))
             for b in range(blocks)
         ],
         1,
@@ -289,13 +313,15 @@
 
         lax.fori_loop(first, past, pack, 0)
 
-        def serve(k, carry):
-            d = peer(me, k, count)
-            span = pl.ds(first, past - first)
-            to_ctx(row_send.at[span, d], row_recv.at[span, me], ROWS + number, d).start()
-            return carry
-
-        lax.fori_loop(1, count, serve, 0)
+        span = pl.ds(first, past - first)
+        spread(
+            me,
+            count,
+            lambda d: to_ctx(
+                row_send.at[span, d], row_recv.at[span, me], ROWS + number, d
+            ).start(),
+        )
+        note(row_send.at[span, others], row_recv.at[span, others], ROWS + number)
 
     def own(h, carry):
         row_recv[h, me] = row_send[h, me]
@@ -340,33 +366,47 @@
             qd = q * eq
             kd = store * ek
             qd2 = halves(qd)
-            scores = nt3(qd2, halves(kd)) * shared_ref[b]
-            out = nn2(halves(scores), v_exact) + valid_ref[b] * nt3(qd2, halves(state))
+            kd2 = halves(kd)
+            state2 = halves(state)
+            scores = nt3(qd2, kd2) * shared_ref[b]
+            out = nn2(halves(scores), v_exact) + valid_ref[b] * nt3(qd2, state2)
+            up = gain * y
+            square_ref[at] += out * out
+            cross_ref[at] += up * out
             state_ref[h, b] = state
             state = state * factor + exact_nn2(v.T.astype(BF), halves(store * tail))
-            square_ref[at] += out * out
-            cross_ref[at] += gain * y * out
+            for value, weight_ref, query_ref, turned_ref in (
+                (up, up_weight_ref, up_query_ref, up_t_ref),
+                (out, out_weight_ref, out_query_ref, out_t_ref),
+            ):
+                value2 = halves(value)
+                weights = nt2(value2, v_exact) * shared_ref[b]
+                query_ref[h, b] = eq * (
+                    nn3(halves(weights), kd2) + valid_ref[b] * nn3(value2, state2)
+                )
+                weight_ref[h, b] = weights.T
+                turned_ref[h, b] = (value * valid_ref[b]).T
             q_bal[h, b] = q.astype(BF)
             v_bal[h, b] = v_exact
             y_bal[h, b] = y.astype(BF)
             sig_ref[h, b] = sig
             forget_ref[h, b] = forget
             store_ref[h, b] = store
-            eq_ref[h, b] = eq
             ek_ref[h, b] = ek
             tail_ref[h, b] = tail
-            qd_ref[h, b] = qd
-            kd_ref[h, b] = kd
-            score_ref[h, b] = scores
+            qd_ref[h, b, 0], qd_ref[h, b, 1] = qd2
+            score_t_ref[h, b, 0], score_t_ref[h, b, 1] = halves(scores.T)
             factor_ref[h, b] = factor
             out_ref[h, b] = out
         state_ref[h, blocks] = state
         return carry
 
     for number, (first, past) in enumerate(chunks):
-        wait_all(
-            row_recv.at[pl.ds(first, past - first), pl.ds(0, count - 1)], ROWS + number
-        )
+        if number + 1 == len(chunks):
+            pass
+        arrive()
+        if number + 1 == len(chunks):
+            pass
         lax.fori_loop(first, past, forward, 0)
 
     ones = jnp.ones((8, 3 * LANES), BF)
@@ -386,25 +426,34 @@
         return carry
 
     lax.fori_loop(1, head_count, share, 0)
+    if head_count > 1:
+        planes = stat_recv.at[pl.ds(0, head_count - 1)]
+        note(planes, planes, STAT)
     stat_recv[plane] = stat_send[...]
     sum_send[...] = jnp.zeros_like(sum_send)
     if head_count > 1:
-        wait_all(stat_recv.at[pl.ds(0, head_count - 1)], STAT)
+        arrive()
     stats = jnp.sum(stat_recv[...], axis=0)
     width = float(head_count * heads * LANES)
     inverse = lax.rsqrt(stats[0:1] / width + EPSILON)
     slope = inverse * inverse * inverse * (stats[4:5] / width)
     square_ref[...] = column(inverse)
     cross_ref[...] = column(slope)
+    scale_ref[0:1] = inverse
+    scale_ref[1:2] = slope
+
+    def pair(ref, h, b):
+        return ref[h, b, 0], ref[h, b, 1]
+
+    def mixed_t(up_part, out_part, b):
+        at = slice(b * BLOCK, (b + 1) * BLOCK)
+        return scale_ref[0:1, at] * up_part - scale_ref[1:2, at] * out_part
 
     def summarize(h, carry):
-        gain = gain_ref[pl.ds(h, 1)]
         back = []
         for b in range(blocks):
-            at = slice(b * BLOCK, (b + 1) * BLOCK)
-            g = square_ref[at] * gain * y_bal[h, b].astype(F32) - out_ref[h, b] * cross_ref[at]
-            out_ref[h, b] = g
-            back.append(nn3(halves((g * valid_ref[b]).T), halves(qd_ref[h, b])))
+            turned = mixed_t(up_t_ref[h, b], out_t_ref[h, b], b)
+            back.append(nn3(halves(turned), pair(qd_ref, h, b)))
             back_state_ref[h, b] = back[b]
         summary = back[blocks - 1]
         decay = factor_ref[h, blocks - 1]
@@ -429,48 +478,37 @@
         return carry
 
     lax.fori_loop(1, group, give_summary, 0)
+    members = pl.ds(0, group - 1)
+    note(sum_send.at[members], sum_recv.at[members], SUM)
     sum_recv[mine] = sum_send[mine]
 
-    def query_side(h, carry):
-        for b in range(blocks):
-            g2 = halves(out_ref[h, b])
-            weights = nt2(g2, v_bal[h, b]) * shared_ref[b]
-            weight_ref[h, b] = weights
-            dq = nn3(halves(weights), halves(kd_ref[h, b]))
-            dq = dq + valid_ref[b] * nn3(g2, halves(state_ref[h, b]))
-            dq_bal[h, b] = dq * eq_ref[h, b]
-        return carry
-
-    lax.fori_loop(0, heads, query_side, 0)
-
-    def column_of(ref, h):
-        return cat([ref[h, b].astype(BF) for b in range(blocks)], 0)
-
-    halfway = (heads + 1) // 2
-    for c in range(halfway):
-        pair = [column_of(dq_bal, c)]
-        if halfway + c < heads:
-            pair.append(column_of(dq_bal, halfway + c))
-        else:
-            pair.append(jnp.zeros((rows, LANES), BF))
-        sent = dot(back_ref[...], cat(pair, 1), NN)
-        slab = cat(
-            [sent[:, a * LANES : (a + 1) * LANES].reshape(count, cap, LANES) for a in range(2)],
-            1,
+    def query_part(first, past, sem):
+        def query_side(h, carry):
+            parts = []
+            for b in range(blocks):
+                at = slice(b * BLOCK, (b + 1) * BLOCK)
+                dq = square_ref[at] * up_query_ref[h, b] - cross_ref[at] * out_query_ref[h, b]
+                dq_bal[h, b] = dq
+                parts.append(dq.astype(BF))
+            away = dot(back_ref[...], cat(parts, 0), NN)
+            dq_send[h] = away.reshape(count, cap, LANES).astype(BF)
+            dq_recv[h, me] = dq_send[h, me]
+            return carry
+
+        lax.fori_loop(first, past, query_side, 0)
+        span = pl.ds(first, past - first)
+        spread(
+            me,
+            count,
+            lambda d: to_ctx(dq_send.at[span, d], dq_recv.at[span, me], sem, d).start(),
         )
-        dq_send[c] = slab.astype(BF)
-
-    def home_queries(k, carry):
-        d = peer(me, k, count)
-        to_ctx(
-            dq_send.at[pl.ds(0, halfway), d], dq_recv.at[pl.ds(0, halfway), me], DQ, d
-        ).start()
-        return carry
-
-    wait_all(sum_recv.at[pl.ds(0, group - 1)], SUM)
-    lax.fori_loop(1, count, home_queries, 0)
-    for c in range(halfway):
-        dq_recv[c, me] = dq_send[c, me]
+        leaving.append((dq_send.at[span, others], sem))
+        return dq_recv.at[span, others], sem
+
+    cuts = [heads * i // 3 for i in range(4)]
+    dq_due = [query_part(cuts[0], cuts[1], DQ)]
+
+    arrive()
 
     def scan(h, carry):
         total = jnp.zeros((part, LANES), F32)
@@ -483,17 +521,11 @@
     groups = count // group
     if groups > 1:
         to_ctx(tot_send, tot_recv, TOT, lax.rem(me + count - group, count)).start()
-
-    def key_side(h, carry):
-        for b in range(blocks):
-            dk_bal[h, b] = ek_ref[h, b] * nn3(
-                halves(weight_ref[h, b].T), halves(qd_ref[h, b])
-            )
-            dv_bal[h, b] = nn3(halves(score_ref[h, b].T), halves(out_ref[h, b]))
-        return carry
+        note(tot_send, tot_recv, TOT)
+    dq_due.append(query_part(cuts[1], cuts[2], DQ + 1))
 
     if groups > 1:
-        wait_all(tot_recv, TOT)
+        arrive()
 
     def carries(h, carry):
         if groups > 1:
@@ -513,9 +545,23 @@
         return carry
 
     lax.fori_loop(1, group, give_carry, 0)
+    note(car_send.at[members], car_recv.at[members], CAR)
     car_recv[mine] = car_send[mine]
+    dq_due.append(query_part(cuts[2], cuts[3], DQ + 2))
+
+    def key_side(h, carry):
+        gain = gain_ref[pl.ds(h, 1)]
+        for b in range(blocks):
+            at = slice(b * BLOCK, (b + 1) * BLOCK)
+            g = square_ref[at] * (gain * y_bal[h, b].astype(F32)) - cross_ref[at] * out_ref[h, b]
+            weights = mixed_t(up_weight_ref[h, b], out_weight_ref[h, b], b)
+            dk_bal[h, b] = ek_ref[h, b] * nn3(halves(weights), pair(qd_ref, h, b))
+            dv_bal[h, b] = nn3(pair(score_t_ref, h, b), halves(g))
+        return carry
+
     lax.fori_loop(0, heads, key_side, 0)
-    wait_all(car_recv.at[pl.ds(0, group - 1)], CAR)
+    arrive()
+    due.extend(dq_due)
 
     def finish(h, carry):
         bound = bound_ref[pl.ds(h, 1)]
@@ -538,9 +584,9 @@
             pairs[b] = cat([dv.astype(BF), dp.astype(BF)], 1)
             if b:
                 incoming = back_state_ref[h, b] + factor_ref[h, b] * incoming
-        sent = dot(back_ref[...], cat(pairs, 0), NN)
+        away = dot(back_ref[...], cat(pairs, 0), NN)
         slab = cat(
-            [sent[:, a * LANES : (a + 1) * LANES].reshape(count, cap, LANES) for a in range(2)],
+            [away[:, a * LANES : (a + 1) * LANES].reshape(count, cap, LANES) for a in range(2)],
             1,
         )
         dvp_send[h] = slab.astype(BF)
@@ -550,46 +596,49 @@
     for number, (first, past) in enumerate(chunks):
         lax.fori_loop(first, past, finish, 0)
 
-        def home(k, carry):
-            d = peer(me, k, count)
-            span = pl.ds(first, past - first)
-            to_ctx(dvp_send.at[span, d], dvp_recv.at[span, me], DVP + number, d).start()
-            return carry
-
-        lax.fori_loop(1, count, home, 0)
-
-    wait_all(dq_recv.at[pl.ds(0, halfway), pl.ds(0, count - 1)], DQ)
-    for c in range(halfway):
-        rows_home = dot(settle_ref[...], unslab(dq_recv[c], 2), NN).astype(BF)
-        for a in range(2):
-            h = c + a * halfway
-            if h < heads:
-                dq_ref[:, h * LANES : (h + 1) * LANES] = rows_home[:, a * LANES : (a + 1) * LANES]
+        span = pl.ds(first, past - first)
+        spread(
+            me,
+            count,
+            lambda d: to_ctx(
+                dvp_send.at[span, d], dvp_recv.at[span, me], DVP + number, d
+            ).start(),
+        )
+        note(dvp_send.at[span, others], dvp_recv.at[span, others], DVP + number)
+
+    def settle_query(h, carry):
+        slab = dq_recv[h].astype(F32).reshape(slots, LANES).astype(BF)
+        at = pl.ds(pl.multiple_of(h * LANES, LANES), LANES)
+        grad_ref[0, :, at] = dot(settle_ref[...], slab, NN).astype(BF)
+        return carry
+
+    for first, past in zip(cuts[:-1], cuts[1:]):
+        arrive()
+        lax.fori_loop(first, past, settle_query, 0)
 
     def settle(h, carry):
         rows_home = dot(settle_ref[...], unslab(dvp_recv[h], 2), NN).astype(BF)
         at = pl.ds(pl.multiple_of(h * LANES, LANES), LANES)
-        dv_ref[:, at] = rows_home[:, :LANES]
-        dp_ref[:, at] = rows_home[:, LANES:]
+        grad_ref[2, :, at] = rows_home[:, :LANES]
+        grad_ref[1, :, at] = rows_home[:, LANES:]
         return carry
 
     for number, (first, past) in enumerate(chunks):
-        span = pl.ds(first, past - first)
-        wait_all(dvp_recv.at[span, pl.ds(0, count - 1)], DVP + number)
+        if number + 1 == len(chunks):
+            pass
+        arrive()
+        if number + 1 == len(chunks):
+            pass
         lax.fori_loop(first, past, settle, 0)
 
-    drain(req_send.at[pl.ds(0, count - 1)], send_sem, REQ)
-    if head_count > 1:
-        drain(stat_recv.at[pl.ds(0, head_count - 1)], send_sem, STAT)
-    drain(sum_send.at[pl.ds(0, group - 1)], send_sem, SUM)
-    if groups > 1:
-        drain(tot_send, send_sem, TOT)
-    drain(car_send.at[pl.ds(0, group - 1)], send_sem, CAR)
-    drain(dq_send.at[pl.ds(0, halfway), pl.ds(0, count - 1)], send_sem, DQ)
-    for number, (first, past) in enumerate(chunks):
-        span = pl.ds(first, past - first)
-        drain(row_send.at[span, pl.ds(0, count - 1)], send_sem, ROWS + number)
-        drain(dvp_send.at[span, pl.ds(0, count - 1)], send_sem, DVP + number)
+    for view, sem in leaving:
+        drain(view, send_sem, sem)
+
+
+def unstack(grad_ref, dq_ref, dp_ref, dv_ref):
+    dq_ref[...] = grad_ref[0]
+    dp_ref[...] = grad_ref[1]
+    dv_ref[...] = grad_ref[2]
 
 
 def body(
@@ -613,20 +662,18 @@
     group = DOC_MOST // rows
     chunks = tuple((h, h + 1) for h in range(heads))
     sizes = (count, head_count, rows, heads, cap, group, chunks)
-    small = jnp.concatenate([row_map, doc_lengths])
-    small = jnp.pad(small, (0, 8 * LANES - small.shape[0])).reshape(8, LANES)
     part = LANES // group
-    halfway = (heads + 1) // 2
     vmem = pltpu.VMEM
     per_block = (heads, blocks, BLOCK, LANES)
-    semaphores = 6 + 2 * len(chunks)
+    split_block = (heads, blocks, 2, BLOCK, LANES)
+    semaphores = 8 + 2 * len(chunks)
     scratch = [
-        vmem((count, cap, LANES), F32),
-        vmem((count, cap, LANES), F32),
+        vmem((count, 1, LANES), F32),
+        vmem((count, 1, LANES), F32),
         vmem((heads, count, 4 * cap, LANES), BF),
         vmem((heads, count, 4 * cap, LANES), BF),
-        vmem((halfway, count, 2 * cap, LANES), BF),
-        vmem((halfway, count, 2 * cap, LANES), BF),
+        vmem((heads, count, cap, LANES), BF),
+        vmem((heads, count, cap, LANES), BF),
         vmem((heads, count, 2 * cap, LANES), BF),
         vmem((heads, count, 2 * cap, LANES), BF),
         vmem((group, heads + 1, part, LANES), F32),
@@ -654,11 +701,15 @@
         vmem(per_block, F32),
         vmem(per_block, F32),
         vmem(per_block, F32),
-        vmem(per_block, F32),
-        vmem(per_block, F32),
-        vmem(per_block, F32),
-        vmem(per_block, F32),
-        vmem(per_block, F32),
+        vmem(split_block, BF),
+        vmem(split_block, BF),
+        vmem(per_block, F32),
+        vmem(per_block, F32),
+        vmem(per_block, F32),
+        vmem(per_block, F32),
+        vmem(per_block, F32),
+        vmem(per_block, F32),
+        vmem((2, rows), F32),
         vmem((heads, blocks + 1, LANES, LANES), F32),
         vmem((heads, blocks, 1, LANES), F32),
         vmem((heads, blocks, LANES, LANES), F32),
@@ -673,17 +724,18 @@
     ]
     whole = pl.BlockSpec(memory_space=pltpu.VMEM)
     shape = jax.ShapeDtypeStruct(query_rows.shape, BF)
-    return pl.pallas_call(
+    grads = pl.pallas_call(
         functools.partial(kernel, sizes),
-        out_shape=(shape, shape, shape),
-        in_specs=[whole] * 8,
-        out_specs=(whole, whole, whole),
+        out_shape=jax.ShapeDtypeStruct((3,) + query_rows.shape, BF),
+        in_specs=[whole] * 9,
+        out_specs=whole,
         scratch_shapes=scratch,
         compiler_params=pltpu.CompilerParams(
             collective_id=0, has_side_effects=True, vmem_limit_bytes=56 << 20
         ),
     )(
-        small,
+        row_map.reshape(blocks, LANES),
+        doc_lengths.reshape(1, doc_lengths.shape[0]),
         query_rows,
         gate_rows,
         value_rows,
@@ -692,6 +744,9 @@
         lower_bound.reshape(heads, LANES),
         norm_gain.reshape(heads, LANES),
     )
+    return pl.pallas_call(
+        unstack, out_shape=(shape, shape, shape), in_specs=[whole], out_specs=(whole,) * 3
+    )(grads)
 
 
 def solution(mesh):

time: 168 us -> 148 us (0.88)
  Pallas kernels: 162 us -> 147 us
  local copies, waits for them, and re-layouts: 4.85 us -> 0 us
    pallas_call x1 -> x2, Pallas kernels: 162 us -> 147 us  [the longest x1 145 us: body(): pl.pallas_call(functools.partial(kernel, sizes), out_shape=jax.ShapeDtype...]
    unnamed x11 -> x0, local copies, waits for them, and re-layouts: 4.25 us -> none
where the time goes in v1:
time: 148 us
  Pallas kernels  147 us (99%)
    pallas_call x1, Pallas kernels, body(): pl.pallas_call(functools.partial(kernel, sizes), out_shape=jax.ShapeDtype...  145 us

profile of v1, /device:TPU:1, one launch (start us, length us, event | category | flops | bytes accessed | tf_op | source)
XLA Modules:
  0.0 147.8 jit_solution(17380843870129159988)
XLA Ops:
  0.6 145.0 %shard_map.112.grad_ref = bf16[3,256,640]{2,1,0:T(8,128)(2,1)} custom-call(s32[2,128]{1,0:T(2,128)} %bitcast.6, s32[1,64]{1,0:T(1,128)} %bitcast.7, bf16[256,640]{1,0:T(8,128)(2,1)} %q_ref.1, bf16[256,640]{1,0:T(8,128)(2,1)} %p_ref.1, bf16[256,640]{1,0:T(8,128)(2,1)} %v_ref.1, bf16[256,640]{1,0:T(8,128)(2,1)} %y_ref.1, f32[1,5,128,128]{3,2,1,0:T(8,128)} %entry_ref.1, ...), custom_call_target="tpu_custom_call" | custom-call | tf_op jit(solution)/shard_map/pallas_call | solution.py:727
  145.6 2.2 %shard_map.113 = (bf16[256,640]{1,0:T(8,128)(2,1)}, bf16[256,640]{1,0:T(8,128)(2,1)}, bf16[256,640]{1,0:T(8,128)(2,1)}) custom-call(bf16[3,256,640]{2,1,0:T(8,128)(2,1)} %shard_map.112.grad_ref), custom_call_target="tpu_custom_call" | custom-call | tf_op jit(solution)/shard_map/pallas_call | solution.py:747

commit v2 on v1

--- a/solution.py
+++ b/solution.py
@@ -105,14 +105,20 @@
     sizes,
     map_ref,
     length_ref,
+    q_hbm,
+    p_hbm,
+    v_hbm,
+    y_hbm,
+    entry_hbm,
+    bound_ref,
+    gain_ref,
+    grad_ref,
     q_ref,
     p_ref,
     v_ref,
     y_ref,
     entry_ref,
-    bound_ref,
-    gain_ref,
-    grad_ref,
+    load_sem,
     req_send,
     req_recv,
     row_send,
@@ -144,9 +150,12 @@
     sig_ref,
     forget_ref,
     store_ref,
+    eq_ref,
     ek_ref,
     tail_ref,
     qd_ref,
+    kd_ref,
+    score_ref,
     score_t_ref,
     up_t_ref,
     out_t_ref,
@@ -198,7 +207,7 @@
         view, sem = due.pop(0)
         drain(view, recv_sem, sem)
 
-    REQ, STAT, SUM, TOT, CAR, DQ, ROWS = 0, 1, 2, 3, 4, 5, 8
+    REQ, STAT, SUM, TOT, CAR, DQ, ROWS = 0, 1, 2, 4, 6, 8, 11
     DVP = ROWS + len(chunks)
 
     barrier = pltpu.get_barrier_semaphore()
@@ -220,6 +229,21 @@
         ),
     )
     lax.fori_loop(1, head_count, greet_plane, 0)
+
+    loads = [
+        pltpu.make_async_copy(src, dst, load_sem.at[at])
+        for at, (src, dst) in enumerate(
+            (
+                (q_hbm, q_ref),
+                (p_hbm, p_ref),
+                (v_hbm, v_ref),
+                (y_hbm, y_ref),
+                (entry_hbm, entry_ref),
+            )
+        )
+    ]
+    for load in loads:
+        load.start()
 
     map_row = cat([map_ref[b : b + 1] for b in range(blocks)], 1).astype(F32)
     source_row = jnp.floor(map_row * (1.0 / rows))
@@ -277,6 +301,8 @@
         last_ref[b] = one(document_col[at] == final)
         through_ref[pl.ds(b, 1)] = one(previous == final)
 
+    for load in loads:
+        load.wait()
     arrive()
     asked = jnp.broadcast_to(req_recv[...], (count, cap, LANES))
     asked = jnp.where(own_lane, asked, 0.0).reshape(slots, LANES).astype(BF)
@@ -367,47 +393,57 @@
             kd = store * ek
             qd2 = halves(qd)
             kd2 = halves(kd)
-            state2 = halves(state)
             scores = nt3(qd2, kd2) * shared_ref[b]
-            out = nn2(halves(scores), v_exact) + valid_ref[b] * nt3(qd2, state2)
-            up = gain * y
+            out = nn2(halves(scores), v_exact) + valid_ref[b] * nt3(qd2, halves(state))
             square_ref[at] += out * out
-            cross_ref[at] += up * out
+            cross_ref[at] += gain * y * out
             state_ref[h, b] = state
             state = state * factor + exact_nn2(v.T.astype(BF), halves(store * tail))
-            for value, weight_ref, query_ref, turned_ref in (
-                (up, up_weight_ref, up_query_ref, up_t_ref),
-                (out, out_weight_ref, out_query_ref, out_t_ref),
-            ):
-                value2 = halves(value)
-                weights = nt2(value2, v_exact) * shared_ref[b]
-                query_ref[h, b] = eq * (
-                    nn3(halves(weights), kd2) + valid_ref[b] * nn3(value2, state2)
-                )
-                weight_ref[h, b] = weights.T
-                turned_ref[h, b] = (value * valid_ref[b]).T
             q_bal[h, b] = q.astype(BF)
             v_bal[h, b] = v_exact
             y_bal[h, b] = y.astype(BF)
             sig_ref[h, b] = sig
             forget_ref[h, b] = forget
             store_ref[h, b] = store
+            eq_ref[h, b] = eq
             ek_ref[h, b] = ek
             tail_ref[h, b] = tail
             qd_ref[h, b, 0], qd_ref[h, b, 1] = qd2
-            score_t_ref[h, b, 0], score_t_ref[h, b, 1] = halves(scores.T)
+            kd_ref[h, b, 0], kd_ref[h, b, 1] = kd2
+            score_ref[h, b] = scores
             factor_ref[h, b] = factor
             out_ref[h, b] = out
         state_ref[h, blocks] = state
         return carry
 
+    def pair(ref, h, b):
+        return ref[h, b, 0], ref[h, b, 1]
+
+    def ahead(h, carry):
+        gain = gain_ref[pl.ds(h, 1)]
+        for b in range(blocks):
+            v_exact = v_bal[h, b]
+            kd2 = pair(kd_ref, h, b)
+            state2 = halves(state_ref[h, b])
+            score_t_ref[h, b, 0], score_t_ref[h, b, 1] = halves(score_ref[h, b].T)
+            for value, weight_ref, query_ref, turned_ref in (
+                (gain * y_bal[h, b].astype(F32), up_weight_ref, up_query_ref, up_t_ref),
+                (out_ref[h, b], out_weight_ref, out_query_ref, out_t_ref),
+            ):
+                value2 = halves(value)
+                weights = nt2(value2, v_exact) * shared_ref[b]
+                query_ref[h, b] = eq_ref[h, b] * (
+                    nn3(halves(weights), kd2) + valid_ref[b] * nn3(value2, state2)
+                )
+                weight_ref[h, b] = weights.T
+                turned_ref[h, b] = (value * valid_ref[b]).T
+        return carry
+
     for number, (first, past) in enumerate(chunks):
-        if number + 1 == len(chunks):
-            pass
         arrive()
-        if number + 1 == len(chunks):
-            pass
         lax.fori_loop(first, past, forward, 0)
+        if number + 1 < len(chunks):
+            lax.fori_loop(first, past, ahead, 0)
 
     ones = jnp.ones((8, 3 * LANES), BF)
     squares = dot(ones, cat(thirds(square_ref[...]), 1), NT)
@@ -430,6 +466,7 @@
         planes = stat_recv.at[pl.ds(0, head_count - 1)]
         note(planes, planes, STAT)
     stat_recv[plane] = stat_send[...]
+    lax.fori_loop(chunks[-1][0], chunks[-1][1], ahead, 0)
     sum_send[...] = jnp.zeros_like(sum_send)
     if head_count > 1:
         arrive()
@@ -442,60 +479,64 @@
     scale_ref[0:1] = inverse
     scale_ref[1:2] = slope
 
-    def pair(ref, h, b):
-        return ref[h, b, 0], ref[h, b, 1]
-
     def mixed_t(up_part, out_part, b):
         at = slice(b * BLOCK, (b + 1) * BLOCK)
         return scale_ref[0:1, at] * up_part - scale_ref[1:2, at] * out_part
 
-    def summarize(h, carry):
-        back = []
-        for b in range(blocks):
-            turned = mixed_t(up_t_ref[h, b], out_t_ref[h, b], b)
-            back.append(nn3(halves(turned), pair(qd_ref, h, b)))
-            back_state_ref[h, b] = back[b]
-        summary = back[blocks - 1]
-        decay = factor_ref[h, blocks - 1]
-        for b in reversed(range(blocks - 1)):
-            summary = back[b] + factor_ref[h, b] * summary
-            decay = decay * factor_ref[h, b]
-        sum_send[:, h] = summary.reshape(group, part, LANES)
-        sum_send[:, heads, pl.ds(h, 1)] = jnp.broadcast_to(decay[None], (group, 1, LANES))
-        return carry
-
-    lax.fori_loop(0, heads, summarize, 0)
-
     first_member = lax.div(me, group) * group
     mine = lax.rem(me, group)
-
-    def member(k):
-        return lax.rem(mine + k, group)
-
-    def give_summary(k, carry):
-        m = member(k)
-        to_ctx(sum_send.at[m], sum_recv.at[mine], SUM, first_member + m).start()
-        return carry
-
-    lax.fori_loop(1, group, give_summary, 0)
+    groups = count // group
     members = pl.ds(0, group - 1)
-    note(sum_send.at[members], sum_recv.at[members], SUM)
+
+    def to_members(view, sem):
+        def give(k, carry):
+            m = lax.rem(mine + k, group)
+            to_ctx(*view(m), sem, first_member + m).start()
+            return carry
+
+        lax.fori_loop(1, group, give, 0)
+
+    waves = ((0, 1), (1, heads))
+    for w, (first, past) in enumerate(waves):
+
+        def summarize(h, carry):
+            back = []
+            for b in range(blocks):
+                turned = mixed_t(up_t_ref[h, b], out_t_ref[h, b], b)
+                back.append(nn3(halves(turned), pair(qd_ref, h, b)))
+                back_state_ref[h, b] = back[b]
+            summary = back[blocks - 1]
+            decay = factor_ref[h, blocks - 1]
+            for b in reversed(range(blocks - 1)):
+                summary = back[b] + factor_ref[h, b] * summary
+                decay = decay * factor_ref[h, b]
+            sum_send[:, h + w] = summary.reshape(group, part, LANES)
+            sum_send[:, past + w, pl.ds(h - first, 1)] = jnp.broadcast_to(
+                decay[None], (group, 1, LANES)
+            )
+            return carry
+
+        lax.fori_loop(first, past, summarize, 0)
+        planes_of = pl.ds(first + w, past - first + 1)
+        to_members(
+            lambda m: (sum_send.at[m, planes_of], sum_recv.at[mine, planes_of]), SUM + w
+        )
+        note(sum_send.at[members, planes_of], sum_recv.at[members, planes_of], SUM + w)
     sum_recv[mine] = sum_send[mine]
 
+    def query_side(h, carry):
+        parts = []
+        for b in range(blocks):
+            at = slice(b * BLOCK, (b + 1) * BLOCK)
+            dq = square_ref[at] * up_query_ref[h, b] - cross_ref[at] * out_query_ref[h, b]
+            dq_bal[h, b] = dq
+            parts.append(dq.astype(BF))
+        away = dot(back_ref[...], cat(parts, 0), NN)
+        dq_send[h] = away.reshape(count, cap, LANES).astype(BF)
+        dq_recv[h, me] = dq_send[h, me]
+        return carry
+
     def query_part(first, past, sem):
-        def query_side(h, carry):
-            parts = []
-            for b in range(blocks):
-                at = slice(b * BLOCK, (b + 1) * BLOCK)
-                dq = square_ref[at] * up_query_ref[h, b] - cross_ref[at] * out_query_ref[h, b]
-                dq_bal[h, b] = dq
-                parts.append(dq.astype(BF))
-            away = dot(back_ref[...], cat(parts, 0), NN)
-            dq_send[h] = away.reshape(count, cap, LANES).astype(BF)
-            dq_recv[h, me] = dq_send[h, me]
-            return carry
-
-        lax.fori_loop(first, past, query_side, 0)
         span = pl.ds(first, past - first)
         spread(
             me,
@@ -505,48 +546,53 @@
         leaving.append((dq_send.at[span, others], sem))
         return dq_recv.at[span, others], sem
 
-    cuts = [heads * i // 3 for i in range(4)]
+    cuts = [0, heads - 2, heads - 1, heads]
+    lax.fori_loop(cuts[0], cuts[1], query_side, 0)
     dq_due = [query_part(cuts[0], cuts[1], DQ)]
 
-    arrive()
-
-    def scan(h, carry):
-        total = jnp.zeros((part, LANES), F32)
-        for m in reversed(range(group)):
-            total = sum_recv[m, h] + sum_recv[m, heads, pl.ds(h, 1)] * total
-        tot_send[h] = total
-        return carry
-
-    lax.fori_loop(0, heads, scan, 0)
-    groups = count // group
-    if groups > 1:
-        to_ctx(tot_send, tot_recv, TOT, lax.rem(me + count - group, count)).start()
-        note(tot_send, tot_recv, TOT)
+    def one_back(m, h, w, total):
+        first, past = waves[w]
+        return sum_recv[m, h + w] + sum_recv[m, past + w, pl.ds(h - first, 1)] * total
+
+    for w, (first, past) in enumerate(waves):
+        arrive()
+
+        def scan(h, carry):
+            total = jnp.zeros((part, LANES), F32)
+            for m in reversed(range(group)):
+                total = one_back(m, h, w, total)
+            tot_send[h] = total
+            return carry
+
+        lax.fori_loop(first, past, scan, 0)
+        if groups > 1:
+            span = pl.ds(first, past - first)
+            before_me = lax.rem(me + count - group, count)
+            to_ctx(tot_send.at[span], tot_recv.at[span], TOT + w, before_me).start()
+            note(tot_send.at[span], tot_recv.at[span], TOT + w)
+    lax.fori_loop(cuts[1], cuts[2], query_side, 0)
     dq_due.append(query_part(cuts[1], cuts[2], DQ + 1))
 
-    if groups > 1:
-        arrive()
-
-    def carries(h, carry):
+    for w, (first, past) in enumerate(waves):
         if groups > 1:
-            total = tot_recv[h] * jnp.where(first_member + group == count, 0.0, 1.0)
-        else:
-            total = jnp.zeros((part, LANES), F32)
-        for m in reversed(range(group)):
-            car_send[m, h] = total
-            total = sum_recv[m, h] + sum_recv[m, heads, pl.ds(h, 1)] * total
-        return carry
-
-    lax.fori_loop(0, heads, carries, 0)
-
-    def give_carry(k, carry):
-        m = member(k)
-        to_ctx(car_send.at[m], car_recv.at[mine], CAR, first_member + m).start()
-        return carry
-
-    lax.fori_loop(1, group, give_carry, 0)
-    note(car_send.at[members], car_recv.at[members], CAR)
+            arrive()
+
+        def carries(h, carry):
+            if groups > 1:
+                total = tot_recv[h] * jnp.where(first_member + group == count, 0.0, 1.0)
+            else:
+                total = jnp.zeros((part, LANES), F32)
+            for m in reversed(range(group)):
+                car_send[m, h] = total
+                total = one_back(m, h, w, total)
+            return carry
+
+        lax.fori_loop(first, past, carries, 0)
+        span = pl.ds(first, past - first)
+        to_members(lambda m: (car_send.at[m, span], car_recv.at[mine, span]), CAR + w)
+        note(car_send.at[members, span], car_recv.at[members, span], CAR + w)
     car_recv[mine] = car_send[mine]
+    lax.fori_loop(cuts[2], cuts[3], query_side, 0)
     dq_due.append(query_part(cuts[2], cuts[3], DQ + 2))
 
     def key_side(h, carry):
@@ -558,10 +604,6 @@
             dk_bal[h, b] = ek_ref[h, b] * nn3(halves(weights), pair(qd_ref, h, b))
             dv_bal[h, b] = nn3(pair(score_t_ref, h, b), halves(g))
         return carry
-
-    lax.fori_loop(0, heads, key_side, 0)
-    arrive()
-    due.extend(dq_due)
 
     def finish(h, carry):
         bound = bound_ref[pl.ds(h, 1)]
@@ -593,18 +635,23 @@
         dvp_recv[h, me] = dvp_send[h, me]
         return carry
 
-    for number, (first, past) in enumerate(chunks):
-        lax.fori_loop(first, past, finish, 0)
-
-        span = pl.ds(first, past - first)
-        spread(
-            me,
-            count,
-            lambda d: to_ctx(
-                dvp_send.at[span, d], dvp_recv.at[span, me], DVP + number, d
-            ).start(),
-        )
-        note(dvp_send.at[span, others], dvp_recv.at[span, others], DVP + number)
+    for w, wave in enumerate(waves):
+        lax.fori_loop(*wave, key_side, 0)
+        arrive()
+        for number, (first, past) in enumerate(chunks):
+            if first < wave[0] or first >= wave[1]:
+                continue
+            lax.fori_loop(first, past, finish, 0)
+            span = pl.ds(first, past - first)
+            spread(
+                me,
+                count,
+                lambda d: to_ctx(
+                    dvp_send.at[span, d], dvp_recv.at[span, me], DVP + number, d
+                ).start(),
+            )
+            note(dvp_send.at[span, others], dvp_recv.at[span, others], DVP + number)
+    due[0:0] = dq_due
 
     def settle_query(h, carry):
         slab = dq_recv[h].astype(F32).reshape(slots, LANES).astype(BF)
@@ -624,21 +671,28 @@
         return carry
 
     for number, (first, past) in enumerate(chunks):
-        if number + 1 == len(chunks):
-            pass
         arrive()
-        if number + 1 == len(chunks):
-            pass
         lax.fori_loop(first, past, settle, 0)
 
     for view, sem in leaving:
         drain(view, send_sem, sem)
 
 
-def unstack(grad_ref, dq_ref, dp_ref, dv_ref):
-    dq_ref[...] = grad_ref[0]
-    dp_ref[...] = grad_ref[1]
-    dv_ref[...] = grad_ref[2]
+def unstack(grad_ref, dq_ref, dp_ref, dv_ref, held, sem):
+    outs = (dq_ref, dp_ref, dv_ref)
+    loads = [
+        pltpu.make_async_copy(grad_ref.at[a], held.at[a], sem.at[a]) for a in range(3)
+    ]
+    stores = [
+        pltpu.make_async_copy(held.at[a], outs[a], sem.at[3 + a]) for a in range(3)
+    ]
+    for load in loads:
+        load.start()
+    for load, store in zip(loads, stores):
+        load.wait()
+        store.start()
+    for store in stores:
+        store.wait()
 
 
 def body(
@@ -666,8 +720,10 @@
     vmem = pltpu.VMEM
     per_block = (heads, blocks, BLOCK, LANES)
     split_block = (heads, blocks, 2, BLOCK, LANES)
-    semaphores = 8 + 2 * len(chunks)
-    scratch = [
+    semaphores = 11 + 2 * len(chunks)
+    scratch = [vmem(query_rows.shape, BF) for _ in range(4)] + [
+        vmem(entry_state.shape, F32),
+        pltpu.SemaphoreType.DMA((5,)),
         vmem((count, 1, LANES), F32),
         vmem((count, 1, LANES), F32),
         vmem((heads, count, 4 * cap, LANES), BF),
@@ -676,8 +732,8 @@
         vmem((heads, count, cap, LANES), BF),
         vmem((heads, count, 2 * cap, LANES), BF),
         vmem((heads, count, 2 * cap, LANES), BF),
-        vmem((group, heads + 1, part, LANES), F32),
-        vmem((group, heads + 1, part, LANES), F32),
+        vmem((group, heads + 2, part, LANES), F32),
+        vmem((group, heads + 2, part, LANES), F32),
         vmem((heads, part, LANES), F32),
         vmem((heads, part, LANES), F32),
         vmem((group, heads, part, LANES), F32),
@@ -701,7 +757,10 @@
         vmem(per_block, F32),
         vmem(per_block, F32),
         vmem(per_block, F32),
+        vmem(per_block, F32),
         vmem(split_block, BF),
+        vmem(split_block, BF),
+        vmem(per_block, F32),
         vmem(split_block, BF),
         vmem(per_block, F32),
         vmem(per_block, F32),
@@ -723,11 +782,12 @@
         pltpu.SemaphoreType.DMA((semaphores,)),
     ]
     whole = pl.BlockSpec(memory_space=pltpu.VMEM)
+    anywhere = pl.BlockSpec(memory_space=pl.ANY)
     shape = jax.ShapeDtypeStruct(query_rows.shape, BF)
     grads = pl.pallas_call(
         functools.partial(kernel, sizes),
         out_shape=jax.ShapeDtypeStruct((3,) + query_rows.shape, BF),
-        in_specs=[whole] * 9,
+        in_specs=[whole] * 2 + [anywhere] * 5 + [whole] * 2,
         out_specs=whole,
         scratch_shapes=scratch,
         compiler_params=pltpu.CompilerParams(
@@ -745,7 +805,14 @@
         norm_gain.reshape(heads, LANES),
     )
     return pl.pallas_call(
-        unstack, out_shape=(shape, shape, shape), in_specs=[whole], out_specs=(whole,) * 3
+        unstack,
+        out_shape=(shape, shape, shape),
+        in_specs=[anywhere],
+        out_specs=(anywhere,) * 3,
+        scratch_shapes=[
+            pltpu.VMEM((3,) + query_rows.shape, BF),
+            pltpu.SemaphoreType.DMA((6,)),
+        ],
     )(grads)
 
 

time: 148 us -> 143 us (0.966)
  Pallas kernels: 147 us -> 142 us
    pallas_call x1, Pallas kernels: 145 us -> 140 us  [body(): pl.pallas_call(functools.partial(kernel, sizes), out_shape=jax.ShapeDtype...]
where the time goes in v2:
time: 143 us
  Pallas kernels  142 us (99%)
    pallas_call x1, Pallas kernels, body(): pl.pallas_call(functools.partial(kernel, sizes), out_shape=jax.ShapeDtype...  140 us

profile of v2, /device:TPU:1, one launch (start us, length us, event | category | flops | bytes accessed | tf_op | source)
XLA Modules:
  0.0 143.0 jit_solution(2951051441555142642)
XLA Ops:
  0.6 140.3 %shard_map.112.grad_ref = bf16[3,256,640]{2,1,0:T(8,128)(2,1)} custom-call(s32[2,128]{1,0:T(2,128)} %bitcast.6, s32[1,64]{1,0:T(1,128)} %bitcast.7, bf16[256,640]{1,0:T(8,128)(2,1)} %q_hbm.1, bf16[256,640]{1,0:T(8,128)(2,1)} %p_hbm.1, bf16[256,640]{1,0:T(8,128)(2,1)} %v_hbm.1, bf16[256,640]{1,0:T(8,128)(2,1)} %y_hbm.1, f32[1,5,128,128]{3,2,1,0:T(8,128)} %entry_hbm.1, ...), custom_call_target="tpu_custom_call" | custom-call | tf_op jit(solution)/shard_map/pallas_call | solution.py:787
  140.9 2.0 %shard_map.113 = (bf16[256,640]{1,0:T(8,128)(2,1)}, bf16[256,640]{1,0:T(8,128)(2,1)}, bf16[256,640]{1,0:T(8,128)(2,1)}) custom-call(bf16[3,256,640]{2,1,0:T(8,128)(2,1)} %shard_map.112.grad_ref), custom_call_target="tpu_custom_call" | custom-call | tf_op jit(solution)/shard_map/pallas_call | solution.py:807
